TPU v7x, 32 devices: a whole 2x2x4 slice. The times are simulated.
32 devices in a mesh: groups: 2 (over x), seq: 4 (over y, core), dp: 4 (over z).
Axes of the slice: x: 2, y: 2, z: 4, core: 2. Of those that a mesh axis runs over, the one named last changes fastest.
Arguments:
- stream_in: bfloat16 [8, 2048, 512], P(('groups', 'dp'), 'seq'), parts along dimension 0, may hold values from -6 to 6
- conv_weight: bfloat16 [2, 1536, 1024], replicated, may hold values from -0.15625 to 0.15625
- res_weight: bfloat16 [2, 512, 512], replicated, may hold values from -0.25 to 0.25
- out_cotangent: bfloat16 [8, 2048, 512], P(('groups', 'dp'), 'seq'), parts along dimension 0, may hold values from -6 to 6
Outputs:
- output: bfloat16 [8, 2048, 512], P(('groups', 'dp'), 'seq'), parts along dimension 0
- input_grad: float32 [8, 2048, 512], P(('groups', 'dp'), 'seq'), parts along dimension 0
- grad_conv: float32 [4, 1536, 1024], P('groups', 'seq', 'dp'), parts along dimension 0
- grad_res: float32 [4, 512, 512], P('groups', 'seq', 'dp'), parts along dimension 0
There are 2 independent parts, one for each index of `groups`. A program takes and returns all parts, laid end to end along the dimension named above; an argument that names none is the same for every part. Nothing has to cross between parts.
All inputs are finite; a program needn't handle non-finite values.
Results may differ from a plain program's by a relative error of at most 0.0055.
Values may be sent and summed in bfloat16 or wider, within the bound.
A program may use at most 128 MiB of HBM per device.

v0:
```python
import jax
import jax.numpy as jnp
from jax import lax
from jax.sharding import PartitionSpec as P

DILATION = 512


def shifted(value, axis, steps):
    count = lax.axis_size(axis)
    leading, last = (max(0, -steps), min(count, count - steps))
    return lax.ppermute(value, axis, [(source, source + steps) for source in range(leading, last)])


def moved_back(values, distance):
    if distance >= lax.axis_size("seq"):
        return jnp.zeros_like(values)
    return shifted(values, "seq", distance)


def moved_ahead(values, distance):
    if distance >= lax.axis_size("seq"):
        return jnp.zeros_like(values)
    return shifted(values, "seq", -distance)


def looking_back(values, offset):
    length = values.shape[1]
    whole_shards, remainder = divmod(offset, length)
    return moved_back(values, whole_shards)


def looking_ahead(values, offset):
    length = values.shape[1]
    whole_shards, remainder = divmod(offset, length)
    return moved_ahead(values, whole_shards)


def spread_sum(left_side, right_side):
    contract = (((0,), (0,)), ((), ()))
    partial_value = lax.psum_scatter(
        lax.dot_general(left_side, right_side, contract, preferred_element_type=jnp.float32),
        "seq",
        scatter_dimension=0,
        tiled=True,
    )
    return lax.psum_scatter(partial_value, "dp", scatter_dimension=1, tiled=True)


def local(stream_in, conv_weight, res_weight, out_cotangent):
    records, length, channels = stream_in.shape
    layer_count = conv_weight.shape[0]
    stream = stream_in
    stored = []
    for layer_index in range(layer_count):
        spacing = DILATION * 4**layer_index
        taps = jnp.concatenate(
            [stream, looking_back(stream, spacing), looking_back(stream, 2 * spacing)], axis=2
        )
        taps_flat = taps.reshape(records * length, 3 * channels)
        preact = jnp.dot(taps_flat, conv_weight[layer_index], preferred_element_type=jnp.float32)
        filter_value = jnp.tanh(preact[:, :channels])
        gate_value = jax.nn.sigmoid(preact[:, channels:])
        gated = (filter_value * gate_value).astype(jnp.bfloat16)
        update = jnp.dot(gated, res_weight[layer_index], preferred_element_type=jnp.float32)
        stream = (
            (stream.reshape(-1, channels).astype(jnp.float32) + update)
            .astype(jnp.bfloat16)
            .reshape(records, length, channels)
        )
        stored.append((taps_flat, filter_value, gate_value, gated))
    stream_grad = out_cotangent.astype(jnp.float32).reshape(-1, channels)
    transpose_rhs = (((1,), (1,)), ((), ()))
    conv_grads = [None] * layer_count
    res_grads = [None] * layer_count
    for layer_index in reversed(range(layer_count)):
        spacing = DILATION * 4**layer_index
        taps_flat, filter_value, gate_value, gated = stored[layer_index]
        signal = stream_grad.astype(jnp.bfloat16)
        res_grads[layer_index] = spread_sum(gated, signal)
        gated_grad = lax.dot_general(
            signal, res_weight[layer_index], transpose_rhs, preferred_element_type=jnp.float32
        )
        filter_grad = gated_grad * gate_value * (1.0 - filter_value * filter_value)
        gate_grad = gated_grad * filter_value * gate_value * (1.0 - gate_value)
        pre_grad = jnp.concatenate([filter_grad, gate_grad], axis=1).astype(jnp.bfloat16)
        conv_grads[layer_index] = spread_sum(taps_flat, pre_grad)
        tap_grads = lax.dot_general(
            pre_grad, conv_weight[layer_index], transpose_rhs, preferred_element_type=jnp.float32
        ).astype(jnp.bfloat16)
        tap_grads = tap_grads.reshape(records, length, 3 * channels)
        first = tap_grads[:, :, :channels].astype(jnp.float32)
        second = looking_ahead(tap_grads[:, :, channels : 2 * channels], spacing).astype(
            jnp.float32
        )
        third = looking_ahead(tap_grads[:, :, 2 * channels :], 2 * spacing).astype(jnp.float32)
        stream_grad = stream_grad + (first + second + third).reshape(-1, channels)
    input_grad = stream_grad.reshape(records, length, channels)
    return (stream, input_grad, jnp.stack(conv_grads), jnp.stack(res_grads))


def solution(mesh):
    placed = (P(("groups", "dp"), "seq", None), P(), P(), P(("groups", "dp"), "seq", None))
    return jax.shard_map(
        local,
        mesh=mesh,
        in_specs=placed,
        out_specs=(
            P(("groups", "dp"), "seq", None),
            P(("groups", "dp"), "seq", None),
            P("groups", "seq", "dp"),
            P("groups", "seq", "dp"),
        ),
        check_vma=False,
    )
```

profile of v0, /device:TPU:4, one launch (start us, length us, event | category | flops | bytes accessed | tf_op | source)
XLA Modules:
  0.0 339.5 jit_solution(2302747960222918593)
XLA Ops:
  7.2 1.9 collective-permute-start
  9.1 1.3 collective-permute-start.1
  10.4 10.5 %collective-permute-done = bf16[1,512,512]{2,1,0:T(8,128)(2,1)S(1)} collective-permute-done((bf16[1,512,512]{2,1,0:T(8,128)(2,1)}, bf16[1,512,512]{2,1,0:T(8,128)(2,1)S(1)}, u32[]{:S(2)}, u32[]{:S(2)}) %collective-permute-start) | collective-permute-done | bytes 524320 | tf_op jit(solution)/shard_map/ppermute | solution.py:12
  21.0 5.1 %collective-permute-done.1 = bf16[1,512,512]{2,1,0:T(8,128)(2,1)S(1)} collective-permute-done((bf16[1,512,512]{2,1,0:T(8,128)(2,1)}, bf16[1,512,512]{2,1,0:T(8,128)(2,1)S(1)}, u32[]{:S(2)}, u32[]{:S(2)}) %collective-permute-start.1) | collective-permute-done | bytes 524320 | tf_op jit(solution)/shard_map/ppermute | solution.py:12
  26.1 4.1 %fusion.6 = f32[512,1024]{1,0:T(8,128)S(1)} fusion(bf16[2,1536,1024]{2,1,0:T(8,128)(2,1)} %param.5, bf16[1,512,512]{2,1,0:T(8,128)(2,1)S(1)} %collective-permute-done.1, bf16[1,512,512]{2,1,0:T(8,128)(2,1)S(1)} %collective-permute-done, bf16[1,512,512]{2,1,0:T(8,128)(2,1)} %param.4), kind=kOutput, calls=%fused_computation.6 | convolution fusion | flops 1615331328 | bytes 6815744 | tf_op jit(solution)/shard_map/dot_general | solution.py:61
  32.1 1.8 fusion.2
  33.9 1.9 multiply_convert_fusion.3
  36.6 1.4 fusion.41
  38.1 4.0 %fusion.18 = bf16[1,512,1536]{2,1,0:T(8,128)(2,1)S(1)} fusion(bf16[2,1536,1024]{2,1,0:T(8,128)(2,1)} %param.5, bf16[512,512]{1,0:T(8,128)(2,1)} %get-tuple-element.7, bf16[512,512]{1,0:T(8,128)(2,1)} %get-tuple-element.6), kind=kOutput, calls=%fused_computation.14 | convolution fusion | flops 1613496320 | bytes 5767168 | tf_op jit(solution)/shard_map/dot_general | solution.py:88
  42.1 1.2 copy-done.1
  43.3 1.5 fusion.54
  44.9 2.1 multiply_convert_fusion.1
  47.1 0.8 copy-done.17
  48.0 4.5 %fusion.39 = f32[1536,1024]{1,0:T(8,128)} fusion(bf16[512,512]{1,0:T(8,128)(2,1)S(1)} %get-tuple-element.5, bf16[512,512]{1,0:T(8,128)(2,1)S(1)} %get-tuple-element.4, bf16[1,512,512]{2,1,0:T(8,128)(2,1)S(1)} %copy-done.12, bf16[1,512,512]{2,1,0:T(8,128)(2,1)S(1)} %copy-done.10, bf16[1,512,512]{2,1,0:T(8,128)(2,1)S(1)} %copy-done.8), kind=kOutput, calls=%fused_computation.49 | convolution fusion | flops 1617428480 | bytes 8912896 | tf_op jit(solution)/shard_map/dot_general | solution.py:42
  52.6 1.0 copy-done.14
  53.9 4.4 %fusion.24 = f32[1536,1024]{1,0:T(8,128)} fusion(bf16[1,512,512]{2,1,0:T(8,128)(2,1)S(1)} %bitcast.77, bf16[512,512]{1,0:T(8,128)(2,1)S(1)} %copy-done.16, bf16[512,512]{1,0:T(8,128)(2,1)S(1)} %copy-done.15), kind=kOutput, calls=%fused_computation.17 | convolution fusion | flops 1612709888 | bytes 7864320 | tf_op jit(solution)/shard_map/dot_general | solution.py:42
  58.4 7.2 %reduce-scatter.21.cloned.1.call-done = f32[128,512]{1,0:T(8,128)} async-done(((f32[512,512]{1,0:T(8,128)}), f32[128,512]{1,0:T(8,128)}) %reduce-scatter.21.cloned.1.call-update) | async-done | bytes 262160 | tf_op jit(solution)/shard_map/reduce_scatter | solution.py:41
  65.7 27.5 %reduce-scatter.17.cloned.1.call-done = f32[128,512]{1,0:T(8,128)} async-done(((f32[512,512]{1,0:T(8,128)}), f32[128,512]{1,0:T(8,128)}) %reduce-scatter.17.cloned.1.call-update) | async-done | bytes 262160 | tf_op jit(solution)/shard_map/reduce_scatter | solution.py:41
  93.3 60.9 %reduce-scatter.9.cloned.1.call-done = f32[384,1024]{1,0:T(8,128)} async-done(((f32[1536,1024]{1,0:T(8,128)}), f32[384,1024]{1,0:T(8,128)}) %reduce-scatter.9.cloned.1.call-update) | async-done | bytes 1572880 | tf_op jit(solution)/shard_map/reduce_scatter | solution.py:41
  154.4 60.7 %reduce-scatter.13.cloned.1.call-done = f32[384,1024]{1,0:T(8,128)} async-done(((f32[1536,1024]{1,0:T(8,128)}), f32[384,1024]{1,0:T(8,128)}) %reduce-scatter.13.cloned.1.call-update) | async-done | bytes 1572880 | tf_op jit(solution)/shard_map/reduce_scatter | solution.py:41
  215.1 3.7 %fusion.21 = bf16[1,512,1536]{2,1,0:T(8,128)(2,1)S(1)} fusion(bf16[2,1536,1024]{2,1,0:T(8,128)(2,1)} %param.5, bf16[512,512]{1,0:T(8,128)(2,1)S(1)} %copy-done.20, bf16[512,512]{1,0:T(8,128)(2,1)S(1)} %copy-done.18), kind=kOutput, calls=%fused_computation.15 | convolution fusion | flops 1613496320 | bytes 5767168 | tf_op jit(solution)/shard_map/dot_general | solution.py:88
  219.0 3.2 collective-permute-start.2
  222.2 1.9 collective-permute-start.3
  224.1 1.2 fusion.31
  225.3 7.1 %collective-permute-done.2 = bf16[1,512,512]{2,1,0:T(8,128)(2,1)S(1)} collective-permute-done((bf16[1,512,512]{2,1,0:T(8,128)(2,1)S(1)}, bf16[1,512,512]{2,1,0:T(8,128)(2,1)S(1)}, u32[]{:S(2)}, u32[]{:S(2)}) %collective-permute-start.2) | collective-permute-done | bytes 524320 | tf_op jit(solution)/shard_map/ppermute | solution.py:12
  232.4 7.7 %collective-permute-done.3 = bf16[1,512,512]{2,1,0:T(8,128)(2,1)S(1)} collective-permute-done((bf16[1,512,512]{2,1,0:T(8,128)(2,1)S(1)}, bf16[1,512,512]{2,1,0:T(8,128)(2,1)S(1)}, u32[]{:S(2)}, u32[]{:S(2)}) %collective-permute-start.3) | collective-permute-done | bytes 524320 | tf_op jit(solution)/shard_map/ppermute | solution.py:12
  240.1 2.3 add_add_fusion
  242.4 15.7 %reduce-scatter.19.cloned.1.call-done = f32[128,128]{1,0:T(8,128)} async-done(((f32[128,512]{1,0:T(8,128)}), f32[128,128]{1,0:T(8,128)}) %reduce-scatter.19.cloned.1.call-update) | async-done | bytes 65552 | tf_op jit(solution)/shard_map/reduce_scatter | solution.py:47
  258.2 1.5 pad_maximum_fusion.7
  259.7 34.3 %reduce-scatter.11.cloned.1.call-done = f32[384,256]{1,0:T(8,128)} async-done(((f32[384,1024]{1,0:T(8,128)}), f32[384,256]{1,0:T(8,128)}) %reduce-scatter.11.cloned.1.call-update) | async-done | bytes 393232 | tf_op jit(solution)/shard_map/reduce_scatter | solution.py:47
  294.0 36.6 %reduce-scatter.15.cloned.1.call-done = f32[384,256]{1,0:T(8,128)} async-done(((f32[384,1024]{1,0:T(8,128)}), f32[384,256]{1,0:T(8,128)}) %reduce-scatter.15.cloned.1.call-update) | async-done | bytes 393232 | tf_op jit(solution)/shard_map/reduce_scatter | solution.py:47
  330.6 2.0 pad_maximum_fusion.2
  (59 shorter events, 3.8 us)
Async XLA Ops:
  7.2 58.5 %reduce-scatter.21.cloned.1.call-start = ((), (), s32[]{:S(2)}) async-start(), calls=%async_computation.14 | async-start | bytes 1310720 | tf_op jit(solution)/shard_map/reduce_scatter | solution.py:41
  7.2 13.8 %collective-permute-start = (bf16[1,512,512]{2,1,0:T(8,128)(2,1)}, bf16[1,512,512]{2,1,0:T(8,128)(2,1)S(1)}, u32[]{:S(2)}, u32[]{:S(2)}) collective-permute-start(bf16[1,512,512]{2,1,0:T(8,128)(2,1)} %param.4), channel_id=1, source_target_pairs={{0,4},{4,8},{8,12},{1,5},{5,9},{9,13},{2,6},{6,10},{10,14},{3,7},{... | collective-permute-start | bytes 1572872 | tf_op jit(solution)/shard_map/ppermute | solution.py:12
  9.1 17.0 %collective-permute-start.1 = (bf16[1,512,512]{2,1,0:T(8,128)(2,1)}, bf16[1,512,512]{2,1,0:T(8,128)(2,1)S(1)}, u32[]{:S(2)}, u32[]{:S(2)}) collective-permute-start(bf16[1,512,512]{2,1,0:T(8,128)(2,1)} %param.4), channel_id=1, source_target_pairs={{0,8},{4,12},{1,9},{5,13},{2,10},{6,14},{3,11},{7,15},{16,24},{20,... | collective-permute-start | bytes 1572872 | tf_op jit(solution)/shard_map/ppermute | solution.py:12
  21.0 5.1 %copy-start.9 = (bf16[1,512,512]{2,1,0:T(8,128)(2,1)}, bf16[1,512,512]{2,1,0:T(8,128)(2,1)S(1)}, u32[]{:S(2)}) copy-start(bf16[1,512,512]{2,1,0:T(8,128)(2,1)S(1)} %collective-permute-done) | copy-start | bytes 1572868
  26.1 4.1 %copy-start.11 = (bf16[1,512,512]{2,1,0:T(8,128)(2,1)}, bf16[1,512,512]{2,1,0:T(8,128)(2,1)S(1)}, u32[]{:S(2)}) copy-start(bf16[1,512,512]{2,1,0:T(8,128)(2,1)S(1)} %collective-permute-done.1) | copy-start | bytes 1572868
  26.1 5.9 %copy-start.4 = (bf16[2,1536,1024]{2,1,0:T(8,128)(2,1)S(1)}, bf16[2,1536,1024]{2,1,0:T(8,128)(2,1)}, u32[]{:S(2)}) copy-start(bf16[2,1536,1024]{2,1,0:T(8,128)(2,1)} %param.5) | copy-start | bytes 18874372
  30.2 1.2 copy-start.5
  30.2 1.3 copy-start.7
  32.0 1.9 copy-start.13
  32.0 1.8 copy-start
  38.0 55.2 %reduce-scatter.17.cloned.1.call-start = ((), (), s32[]{:S(2)}) async-start(), calls=%async_computation.12 | async-start | bytes 1310720 | tf_op jit(solution)/shard_map/reduce_scatter | solution.py:41
  42.1 1.2 copy-start.1
  44.8 3.2 copy-start.8
  44.8 109.4 %reduce-scatter.9.cloned.1.call-start = ((), (), s32[]{:S(2)}) async-start(), calls=%async_computation.8 | async-start | bytes 7864320 | tf_op jit(solution)/shard_map/reduce_scatter | solution.py:41
  44.9 3.2 copy-start.10
  44.9 3.2 copy-start.12
  47.0 0.8 copy-start.17
  47.0 1.0 copy-start.19
  52.5 1.0 copy-start.14
  52.5 1.2 copy-start.15
  52.5 1.4 copy-start.16
  52.6 162.5 %reduce-scatter.13.cloned.1.call-start = ((), (), s32[]{:S(2)}) async-start(), calls=%async_computation.10 | async-start | bytes 7864320 | tf_op jit(solution)/shard_map/reduce_scatter | solution.py:41
  58.3 156.8 %copy-start.18 = (bf16[512,512]{1,0:T(8,128)(2,1)S(1)}, bf16[512,512]{1,0:T(8,128)(2,1)}, u32[]{:S(2)}) copy-start(bf16[512,512]{1,0:T(8,128)(2,1)} %copy-done.17) | copy-start | bytes 1572868
  58.4 156.8 %copy-start.20 = (bf16[512,512]{1,0:T(8,128)(2,1)S(1)}, bf16[512,512]{1,0:T(8,128)(2,1)}, u32[]{:S(2)}) copy-start(bf16[512,512]{1,0:T(8,128)(2,1)} %copy-done.19) | copy-start | bytes 1572868
  58.4 184.1 %reduce-scatter.23.cloned.1.call-start = ((), (), s32[]{:S(2)}) async-start(), calls=%async_computation.15 | async-start | bytes 327680 | tf_op jit(solution)/shard_map/reduce_scatter | solution.py:47
  65.7 192.5 %reduce-scatter.19.cloned.1.call-start = ((), (), s32[]{:S(2)}) async-start(), calls=%async_computation.13 | async-start | bytes 327680 | tf_op jit(solution)/shard_map/reduce_scatter | solution.py:47
  93.3 200.7 %reduce-scatter.11.cloned.1.call-start = ((), (), s32[]{:S(2)}) async-start(), calls=%async_computation.9 | async-start | bytes 1966080 | tf_op jit(solution)/shard_map/reduce_scatter | solution.py:47
  154.2 176.4 %reduce-scatter.15.cloned.1.call-start = ((), (), s32[]{:S(2)}) async-start(), calls=%async_computation.11 | async-start | bytes 1966080 | tf_op jit(solution)/shard_map/reduce_scatter | solution.py:47
  218.9 5.2 %copy-start.3 = (bf16[512,512]{1,0:T(8,128)(2,1)S(1)}, bf16[512,512]{1,0:T(8,128)(2,1)}, u32[]{:S(2)}) copy-start(bf16[512,512]{1,0:T(8,128)(2,1)} %copy-done.2) | copy-start | bytes 1572868
  218.9 5.2 %copy-start.6 = (bf16[2,512,512]{2,1,0:T(8,128)(2,1)S(1)}, bf16[2,512,512]{2,1,0:T(8,128)(2,1)}, u32[]{:S(2)}) copy-start(bf16[2,512,512]{2,1,0:T(8,128)(2,1)} %param.6) | copy-start | bytes 3145732
  219.0 13.4 %collective-permute-start.2 = (bf16[1,512,512]{2,1,0:T(8,128)(2,1)S(1)}, bf16[1,512,512]{2,1,0:T(8,128)(2,1)S(1)}, u32[]{:S(2)}, u32[]{:S(2)}) collective-permute-start(bf16[1,512,512]{2,1,0:T(8,128)(2,1)S(1)} %get-tuple-element.9), channel_id=1, source_target_pairs={{4,0},{8,4},{12,8},{5,1},{9,5},{13,9},{6,2},{10,6},{14,10},{7,3},{... | collective-permute-start | bytes 1572872 | tf_op jit(solution)/shard_map/ppermute | solution.py:12
  222.2 17.9 %collective-permute-start.3 = (bf16[1,512,512]{2,1,0:T(8,128)(2,1)S(1)}, bf16[1,512,512]{2,1,0:T(8,128)(2,1)S(1)}, u32[]{:S(2)}, u32[]{:S(2)}) collective-permute-start(bf16[1,512,512]{2,1,0:T(8,128)(2,1)S(1)} %get-tuple-element.10), channel_id=1, source_target_pairs={{8,0},{12,4},{9,1},{13,5},{10,2},{14,6},{11,3},{15,7},{24,16},{28,... | collective-permute-start | bytes 1572872 | tf_op jit(solution)/shard_map/ppermute | solution.py:12
  (1 other events, 0.8 us)
Sparse Core Ops, SparseCore 0:
  38.1 27.4 reduce-scatter.20
  68.3 24.8 reduce-scatter.16
  95.8 58.3 reduce-scatter.8
  156.7 58.3 reduce-scatter.12
  217.2 20.8 reduce-scatter.22
  240.3 17.8 reduce-scatter.18
  260.5 33.4 reduce-scatter.10
  296.3 34.2 reduce-scatter.14
where the time goes:
time: 341 us; the launch traced here: 339 us
  waiting for transfers between devices  273 us (80%)
  matrix products  31.2 us (9%)
  between operations  14.4 us (4%)
  starting transfers between devices  8.81 us (3%)
  other arithmetic  6.32 us (2%)
  local copies, waits for them, and re-layouts  5.24 us (2%)
    reduce_scatter x4, waiting for transfers between devices, spread_sum(): lax.psum_scatter(lax.dot_general(left_side, right_side, contract, preferr...  156 us
    reduce_scatter x4, waiting for transfers between devices, spread_sum(): lax.psum_scatter(partial_value, 'dp', scatter_dimension=1, tiled=True)  86.6 us
    ppermute x4, waiting for transfers between devices, shifted(): lax.ppermute(value, axis, [(source, source + steps) for source in range(l...  30.4 us
    dot_general x4, matrix products, spread_sum(): lax.dot_general(left_side, right_side, contract, preferred_element_type=j...  11.9 us
    ppermute x4, starting transfers between devices, shifted(): lax.ppermute(value, axis, [(source, source + steps) for source in range(l...  8.31 us
    dot_general x2, matrix products, local(): lax.dot_general(pre_grad, conv_weight[layer_index], transpose_rhs, prefer...  7.76 us
  transfers between devices with their start and end apart: 12, of which 11 were waited for; matrix products, arithmetic and copies ran while one was open for 8% of the time, Pallas kernels for 0%

commit v1 on v0

--- a/solution.py
+++ b/solution.py
@@ -1,6 +1,10 @@
+import functools
+
 import jax
 import jax.numpy as jnp
 from jax import lax
+from jax.experimental import pallas as pl
+from jax.experimental.pallas import tpu as pltpu
 from jax.sharding import PartitionSpec as P
 
 DILATION = 512
@@ -99,10 +103,454 @@
     return (stream, input_grad, jnp.stack(conv_grads), jnp.stack(res_grads))
 
 
+BF16 = jnp.bfloat16
+F32 = jnp.float32
+MESH = pl.DeviceIdType.MESH
+
+
+def mm(left, right):
+    return jnp.dot(left, right, preferred_element_type=F32)
+
+
+def mm_nt(left, right):
+    return lax.dot_general(left, right, (((1,), (1,)), ((), ())), preferred_element_type=F32)
+
+
+def mm_tn(left, right):
+    return lax.dot_general(left, right, (((0,), (0,)), ((), ())), preferred_element_type=F32)
+
+
+def fused_kernel(
+    dp_count,
+    x_ref, w_ref, r_ref, ct_ref,
+    out_ref, ig_ref, gc_ref, gr_ref,
+    sbuf, w0, w1, rw, ctb,
+    fa0, fb0, fa1, fb1, z0, z1, s1, dpre, g1, lt,
+    outv, igv, hsend, hrecv,
+    acc0, acc1, accr,
+    cs0, cr0, cs1, cr1, csr, crr,
+    zs0, zr0, zs1, zr1, zsr, zrr,
+    fs1, fr1, gcv, grv,
+    lsem, osem, ys_s, ys_r, yc_s, yc_r, xs_s, xs_r, fw_s, fw_r, h_s, h_r,
+    c0_s, c0_r, c1_s, c1_r, cr_s, cr_r,
+    za_s, za_r, zb_s, zb_r, zc_s, zc_r, f_s, f_r,
+):
+    s = lax.axis_index("seq")
+    p = lax.axis_index("dp")
+    y = s // 2
+    c = s % 2
+    other = s + 1 - 2 * c
+    across = s + 2 - 4 * y
+    length, chan = x_ref.shape[1], x_ref.shape[2]
+    half = length // 2
+    width = 2 * chan
+    col = width // dp_count
+    rcol = chan // dp_count
+    own0 = 3 * chan // 4
+    own1 = chan // 4
+    ymid = pl.multiple_of(y * (chan // 2), 256)
+
+    local_copies = [
+        pltpu.make_async_copy(x_ref.at[0], sbuf.at[2 + s], lsem.at[0]),
+        pltpu.make_async_copy(w_ref.at[0], w0, lsem.at[1]),
+        pltpu.make_async_copy(r_ref, rw, lsem.at[2]),
+        pltpu.make_async_copy(w_ref.at[1, pl.ds(0, chan)], w1, lsem.at[3]),
+        pltpu.make_async_copy(ct_ref.at[0], ctb.at[0], lsem.at[4]),
+    ]
+    for copy in local_copies:
+        copy.start()
+
+    barrier = pltpu.get_barrier_semaphore()
+    peers = [{"seq": other}, {"seq": across}]
+    peers += [{"dp": (p + k) % dp_count} for k in range(1, dp_count)]
+    for peer in peers:
+        pl.semaphore_signal(barrier, inc=1, device_id=peer, device_id_type=MESH)
+    pl.semaphore_wait(barrier, len(peers))
+
+    def remote(src, dst, send, recv, device):
+        return pltpu.make_async_remote_copy(
+            src_ref=src, dst_ref=dst, send_sem=send, recv_sem=recv,
+            device_id=device, device_id_type=MESH,
+        )
+
+    def rows(h):
+        return pl.ds(h * half, half)
+
+    s_over = [
+        remote(x_ref.at[0, rows(h)], sbuf.at[2 + s, rows(h)], ys_s.at[h], ys_r.at[h], {"seq": across})
+        for h in range(2)
+    ]
+    c_over = [
+        remote(ct_ref.at[0, rows(h)], ctb.at[1, rows(h)], yc_s.at[h], yc_r.at[h], {"seq": across})
+        for h in range(2)
+    ]
+    s_pair = remote(x_ref.at[0], sbuf.at[2 + s], xs_s, xs_r, {"seq": other})
+    s_fwd = [
+        remote(sbuf.at[2 + across, rows(h)], sbuf.at[2 + across, rows(h)], fw_s.at[h], fw_r.at[h],
+               {"seq": other})
+        for h in range(2)
+    ]
+    for h in range(2):
+        s_over[h].start()
+    s_pair.start()
+    for h in range(2):
+        c_over[h].start()
+
+    sbuf[pl.ds(0, 2)] = jnp.zeros((2, length, chan), BF16)
+
+    @pl.when(c == 0)
+    def _():
+        hsend[...] = jnp.zeros_like(hsend)
+
+    for copy in local_copies:
+        copy.wait()
+    s_pair.wait_recv()
+
+    def take_over():
+        for h in range(2):
+            s_over[h].wait_recv()
+            s_fwd[h].start()
+        for h in range(2):
+            s_fwd[h].wait_recv()
+
+    pl.when(y == 1)(take_over)
+
+    def forward(k, u):
+        def part(h, _):
+            r = pl.ds(pl.multiple_of(h * half, half), half)
+            now, back, back2 = sbuf[u + 2, r], sbuf[u + 1, r], sbuf[u, r]
+
+            def pre(lo):
+                return (
+                    mm(now, w0[0:chan, lo : lo + chan])
+                    + mm(back, w0[chan : 2 * chan, lo : lo + chan])
+                    + mm(back2, w0[2 * chan :, lo : lo + chan])
+                )
+
+            def gate(filt, sig, fa, fb):
+                f = jnp.tanh(filt)
+                g = 0.5 * jnp.tanh(0.5 * sig) + 0.5
+                fa[r] = g * (1.0 - f * f)
+                fg = f * g
+                fb[r] = fg * (1.0 - g)
+                return fg.astype(BF16)
+
+            z = gate(pre(0), pre(chan), fa0, fb0)
+            z0[r] = z
+            nxt = (now.astype(F32) + mm(z, rw[0])).astype(BF16)
+            s1[r] = nxt
+            z = gate(mm(nxt, w1[:, 0:chan]), mm(nxt, w1[:, chan:]), fa1, fb1)
+            z1[r] = z
+            if k == 0:
+                outv[r] = (nxt.astype(F32) + mm(z, rw[1])).astype(BF16)
+            return 0
+
+        lax.fori_loop(0, 2, part, 0)
+
+    def transposed(u):
+        lt[pl.ds(ymid, chan)] = sbuf[u + 2 * (1 - y)].T
+        small = sbuf[u + 1, :, pl.ds(ymid, chan // 2)]
+        lt[pl.ds(pl.multiple_of((1 - y) * chan, 256), chan // 2)] = small.T
+
+    def back_one(k, u):
+        def part(h, _):
+            r = pl.ds(pl.multiple_of(h * half, half), half)
+            if k == 1:
+                for hh in range(2):
+                    @pl.when(h == hh)
+                    def _():
+                        c_over[hh].wait_recv()
+            e = ctb[k, r]
+            dz = mm_nt(e, rw[1])
+            df = (dz * fa1[r]).astype(BF16)
+            dg = (dz * fb1[r]).astype(BF16)
+            dpre[r, 0:chan] = df
+            dpre[r, chan:] = dg
+            g1[r] = e.astype(F32) + mm_nt(df, w1[:, 0:chan]) + mm_nt(dg, w1[:, chan:])
+            return 0
+
+        lax.fori_loop(0, 2, part, 0)
+        gr1 = mm_tn(z1[:, pl.ds(ymid, chan // 2)], ctb[k])
+        gc1 = mm_tn(s1[:, pl.ds(ymid, chan // 2)], dpre[...])
+        if k == 0:
+            accr[1] = gr1
+            acc1[...] = gc1
+        else:
+            accr[1] = accr[1] + gr1
+            acc1[...] = acc1[...] + gc1
+
+    def back_zero(k, u):
+        def part(h, _):
+            r = pl.ds(pl.multiple_of(h * half, half), half)
+            dz = mm_nt(g1[r].astype(BF16), rw[0])
+            dpre[r, 0:chan] = (dz * fa0[r]).astype(BF16)
+            dpre[r, chan:] = (dz * fb0[r]).astype(BF16)
+            return 0
+
+        lax.fori_loop(0, 2, part, 0)
+        gr0 = mm_tn(z0[:, pl.ds(ymid, chan // 2)], g1[...].astype(BF16))
+        if k == 0:
+            accr[0] = gr0
+        else:
+            accr[0] = accr[0] + gr0
+
+    def taps_back(lag):
+        def at(r):
+            return mm_nt(dpre[r], w0[lag * chan : (lag + 1) * chan])
+
+        return at
+
+    def over_halves(body):
+        def part(h, _):
+            body(pl.ds(pl.multiple_of(h * half, half), half))
+            return 0
+
+        lax.fori_loop(0, 2, part, 0)
+
+    forward(0, s)
+    out_copy = pltpu.make_async_copy(outv, out_ref.at[0], osem.at[0])
+    out_copy.start()
+    back_one(0, s)
+    back_zero(0, s)
+    transposed(s)
+    for k in range(dp_count):
+        q = (p + k) % dp_count
+        acc0[k] = mm(lt[...], dpre[:, pl.ds(pl.multiple_of(q * col, col), col)])
+
+    def direct(r):
+        igv[r] = g1[r] + taps_back(0)(r)
+
+    over_halves(direct)
+
+    def lagged(r):
+        hsend[r] = taps_back(1)(r).astype(BF16)
+
+    @pl.when(c == 1)
+    def _():
+        over_halves(lagged)
+
+    pl.when(y == 0)(take_over)
+    forward(1, across)
+    transposed(across)
+    back_one(1, across)
+
+    mine1, theirs1 = pl.multiple_of(c * own1, 128), pl.multiple_of((1 - c) * own1, 128)
+    mine0, theirs0 = pl.multiple_of(c * own0, 128), pl.multiple_of((1 - c) * own0, 128)
+
+    def pair_res(layer):
+        return remote(csr.at[layer], crr.at[layer], cr_s.at[layer], cr_r.at[layer], {"seq": other})
+
+    cs1[...] = acc1[pl.ds(theirs1, own1)].astype(BF16)
+    pair1 = remote(cs1, cr1, c1_s, c1_r, {"seq": other})
+    pair1.start()
+    csr[1] = accr[1, pl.ds(theirs1, own1)].astype(BF16)
+    pair_r1 = pair_res(1)
+    pair_r1.start()
+
+    back_zero(1, across)
+
+    def spread(k, src, dst, send, recv):
+        return remote(src, dst, send, recv, {"dp": (p + k) % dp_count})
+
+    def send_res(layer):
+        total = accr[layer, pl.ds(mine1, own1)] + crr[layer].astype(F32)
+        accr[layer, pl.ds(mine1, own1)] = total
+        copies = []
+        for k in range(1, dp_count):
+            q = (p + k) % dp_count
+            part = accr[layer, pl.ds(mine1, own1), pl.ds(pl.multiple_of(q * rcol, rcol), rcol)]
+            zsr[layer, k - 1] = part.astype(BF16)
+            copy = spread(k, zsr.at[layer, k - 1], zrr.at[layer, k - 1], zc_s.at[layer, k - 1],
+                          zc_r.at[layer, k - 1])
+            copy.start()
+            copies.append(copy)
+        return copies
+
+    pair1.wait_recv()
+    acc1[pl.ds(mine1, own1)] = acc1[pl.ds(mine1, own1)] + cr1[...].astype(F32)
+    over1 = []
+    for k in range(1, dp_count):
+        q = (p + k) % dp_count
+        part = acc1[pl.ds(mine1, own1), pl.ds(pl.multiple_of(q * col, col), col)]
+        zs1[k - 1] = part.astype(BF16)
+        copy = spread(k, zs1.at[k - 1], zr1.at[k - 1], zb_s.at[k - 1], zb_r.at[k - 1])
+        copy.start()
+        over1.append(copy)
+    pair_r1.wait_recv()
+    over_r1 = send_res(1)
+
+    csr[0] = accr[0, pl.ds(theirs1, own1)].astype(BF16)
+    pair_r0 = pair_res(0)
+    pair_r0.start()
+
+    order = list(range(1, dp_count)) + [0]
+    pairs0 = {}
+    over0 = []
+
+    def pass_on(k):
+        pairs0[k].wait_recv()
+        if k == 0:
+            return
+        zs0[k - 1] = (acc0[k, pl.ds(mine0, own0)] + cr0[k].astype(F32)).astype(BF16)
+        copy = spread(k, zs0.at[k - 1], zr0.at[k - 1], za_s.at[k - 1], za_r.at[k - 1])
+        copy.start()
+        over0.append(copy)
+
+    for place, k in enumerate(order):
+        q = (p + k) % dp_count
+        acc0[k] = acc0[k] + mm(lt[...], dpre[:, pl.ds(pl.multiple_of(q * col, col), col)])
+        cs0[k] = acc0[k, pl.ds(theirs0, own0)].astype(BF16)
+        pairs0[k] = remote(cs0.at[k], cr0.at[k], c0_s.at[k], c0_r.at[k], {"seq": other})
+        pairs0[k].start()
+        if place > 0:
+            pass_on(order[place - 1])
+    pair_r0.wait_recv()
+    over_r0 = send_res(0)
+
+    @pl.when(jnp.logical_and(c == 0, y == 0))
+    def _():
+        over_halves(lagged)
+
+    pair_h = remote(hsend, hrecv, h_s, h_r, {"seq": other})
+    pair_h.start()
+
+    def lagged_twice(r):
+        igv[r] = igv[r] + taps_back(2)(r)
+
+    @pl.when(y == 0)
+    def _():
+        over_halves(lagged_twice)
+
+    pass_on(0)
+    pair_h.wait_recv()
+    igv[...] = igv[...] + hrecv[...].astype(F32)
+    ig_copy = pltpu.make_async_copy(igv, ig_ref.at[0], osem.at[1])
+    ig_copy.start()
+
+    for copy in over1:
+        copy.wait_recv()
+    here = pl.ds(pl.multiple_of(p * col, col), col)
+    total1 = acc1[pl.ds(mine1, own1), here]
+    for k in range(dp_count - 1):
+        total1 = total1 + zr1[k].astype(F32)
+    fs1[...] = total1
+
+    to_first = remote(fs1, fr1.at[0], f_s, f_r.at[0], {"seq": 0})
+    to_first2 = remote(fs1, fr1.at[1], f_s, f_r.at[1], {"seq": 0})
+    to_second = remote(fs1, fr1.at[0], f_s, f_r.at[0], {"seq": 1})
+    pl.when(s == 1)(to_first.start)
+    pl.when(s == 2)(to_first2.start)
+    pl.when(s == 3)(to_second.start)
+
+    for layer, copies in ((1, over_r1), (0, over_r0)):
+        for copy in copies:
+            copy.wait_recv()
+        total = accr[layer, pl.ds(mine1, own1), pl.ds(pl.multiple_of(p * rcol, rcol), rcol)]
+        for k in range(dp_count - 1):
+            total = total + zrr[layer, k].astype(F32)
+        grv[layer] = total
+    gr_copy = pltpu.make_async_copy(grv, gr_ref, osem.at[2])
+    gr_copy.start()
+
+    gcv[1] = jnp.zeros((own0, col), F32)
+
+    @pl.when(s == 0)
+    def _():
+        gcv[1, 0:own1] = fs1[...]
+        to_first.wait_recv()
+        gcv[1, own1 : 2 * own1] = fr1[0]
+        to_first2.wait_recv()
+        gcv[1, 2 * own1 : 3 * own1] = fr1[1]
+
+    @pl.when(s == 1)
+    def _():
+        to_second.wait_recv()
+        gcv[1, 0:own1] = fr1[0]
+
+    total0 = acc0[0, pl.ds(mine0, own0)] + cr0[0].astype(F32)
+    for k in range(dp_count - 1):
+        over0[k].wait_recv()
+        total0 = total0 + zr0[k].astype(F32)
+    gcv[0] = total0
+    gc_copy = pltpu.make_async_copy(gcv, gc_ref, osem.at[3])
+    gc_copy.start()
+
+    for copy in s_over + c_over + [s_pair] + s_fwd + [pair1, pair_r1, pair_r0, pair_h]:
+        copy.wait_send()
+    for copy in list(pairs0.values()) + over1 + over_r1 + over_r0 + over0:
+        copy.wait_send()
+    pl.when(s > 0)(to_first.wait_send)
+    for copy in (out_copy, ig_copy, gr_copy, gc_copy):
+        copy.wait()
+
+
+def fused(dp_count, stream_in, conv_weight, res_weight, out_cotangent):
+    length, chan = stream_in.shape[1:]
+    width, col, rcol = 2 * chan, 2 * chan // dp_count, chan // dp_count
+    own0, own1 = 3 * chan // 4, chan // 4
+    away = dp_count - 1
+    v = pltpu.VMEM
+    dma = pltpu.SemaphoreType.DMA
+    return pl.pallas_call(
+        functools.partial(fused_kernel, dp_count),
+        out_shape=(
+            jax.ShapeDtypeStruct((1, length, chan), BF16),
+            jax.ShapeDtypeStruct((1, length, chan), F32),
+            jax.ShapeDtypeStruct((2, own0, col), F32),
+            jax.ShapeDtypeStruct((2, own1, rcol), F32),
+        ),
+        in_specs=[pl.BlockSpec(memory_space=pl.ANY)] * 4,
+        out_specs=(pl.BlockSpec(memory_space=pl.ANY),) * 4,
+        scratch_shapes=[
+            v((6, length, chan), BF16), v((3 * chan, width), BF16), v((chan, width), BF16),
+            v((2, chan, chan), BF16), v((2, length, chan), BF16),
+            v((length, chan), F32), v((length, chan), F32), v((length, chan), F32),
+            v((length, chan), F32), v((length, chan), BF16), v((length, chan), BF16),
+            v((length, chan), BF16), v((length, width), BF16), v((length, chan), F32),
+            v((3 * chan // 2, length), BF16),
+            v((length, chan), BF16), v((length, chan), F32),
+            v((length, chan), BF16), v((length, chan), BF16),
+            v((dp_count, 2 * own0, col), F32), v((2 * own1, width), F32), v((2, 2 * own1, chan), F32),
+            v((dp_count, own0, col), BF16), v((dp_count, own0, col), BF16),
+            v((own1, width), BF16), v((own1, width), BF16),
+            v((2, own1, chan), BF16), v((2, own1, chan), BF16),
+            v((away, own0, col), BF16), v((away, own0, col), BF16),
+            v((away, own1, col), BF16), v((away, own1, col), BF16),
+            v((2, away, own1, rcol), BF16), v((2, away, own1, rcol), BF16),
+            v((own1, col), F32), v((2, own1, col), F32),
+            v((2, own0, col), F32), v((2, own1, rcol), F32),
+            dma((5,)), dma((4,)), dma((2,)), dma((2,)), dma((2,)), dma((2,)), dma, dma,
+            dma((2,)), dma((2,)), dma, dma,
+            dma((dp_count,)), dma((dp_count,)), dma, dma, dma((2,)), dma((2,)),
+            dma((away,)), dma((away,)), dma((away,)), dma((away,)),
+            dma((2, away)), dma((2, away)), dma, dma((2,)),
+        ],
+        compiler_params=pltpu.CompilerParams(
+            collective_id=0, has_side_effects=True, vmem_limit_bytes=50 * 1024 * 1024
+        ),
+        cost_estimate=pl.CostEstimate(flops=14 * 10**9, bytes_accessed=12 * 10**6, transcendentals=4 * 10**6),
+    )(stream_in, conv_weight, res_weight, out_cotangent)
+
+
+def dispatch(seq_count, dp_count, stream_in, conv_weight, res_weight, out_cotangent):
+    records, length, channels = stream_in.shape
+    fits = (
+        seq_count == 4
+        and dp_count == 4
+        and records == 1
+        and length == DILATION
+        and channels == 512
+        and conv_weight.shape[0] == 2
+    )
+    if fits:
+        return fused(dp_count, stream_in, conv_weight, res_weight, out_cotangent)
+    return local(stream_in, conv_weight, res_weight, out_cotangent)
+
+
 def solution(mesh):
     placed = (P(("groups", "dp"), "seq", None), P(), P(), P(("groups", "dp"), "seq", None))
     return jax.shard_map(
-        local,
+        functools.partial(dispatch, mesh.shape["seq"], mesh.shape["dp"]),
         mesh=mesh,
         in_specs=placed,
         out_specs=(

time: 341 us -> 71.7 us (0.21)
  waiting for transfers between devices: 273 us -> 0 us
  Pallas kernels: 0 us -> 65.4 us
  matrix products: 31.2 us -> 0 us
  between operations: 14.4 us -> 0.65 us
  starting transfers between devices: 8.81 us -> 0 us
  other arithmetic: 6.32 us -> 0 us
    reduce_scatter x8 -> x0, waiting for transfers between devices: 243 us -> none  [the longest x4 156 us: spread_sum(): lax.psum_scatter(lax.dot_general(left_side, right_side, contract, preferr...]
    pallas_call x0 -> x1, Pallas kernels: none -> 65.4 us  [fused(): pl.pallas_call(functools.partial(fused_kernel, dp_count), out_shape=(jax....]
    dot_general x12 -> x0, matrix products: 31.2 us -> none  [the longest x4 11.9 us: spread_sum(): lax.dot_general(left_side, right_side, contract, preferred_element_type=j...]
    ppermute x4 -> x0, waiting for transfers between devices: 30.4 us -> none  [shifted(): lax.ppermute(value, axis, [(source, source + steps) for source in range(l...]
    ppermute x4 -> x0, starting transfers between devices: 8.31 us -> none  [shifted(): lax.ppermute(value, axis, [(source, source + steps) for source in range(l...]
    another operation x2 -> x0, other arithmetic: 3.58 us -> none  [local(): return (stream, input_grad, jnp.stack(conv_grads), jnp.stack(res_grads))]
  transfers between devices with their start and end apart: 12 -> 0, of which waited for: 11 -> 0; matrix products, arithmetic and copies ran while one was open for 8% -> 0% of each run, Pallas kernels for 0% -> 0%
where the time goes in v1:
time: 71.7 us; the launch traced here: 71.5 us
  Pallas kernels  65.4 us (91%)
  local copies, waits for them, and re-layouts  5.37 us (7%)
    pallas_call x1, Pallas kernels, fused(): pl.pallas_call(functools.partial(fused_kernel, dp_count), out_shape=(jax....  65.4 us
    unnamed x8, local copies, waits for them, and re-layouts  5.37 us

profile of v1, /device:TPU:4, one launch (start us, length us, event | category | flops | bytes accessed | tf_op | source)
XLA Modules:
  0.0 71.5 jit_solution(14315563634456231735)
XLA Ops:
  0.6 0.0 copy-start
  0.6 1.0 %copy-done = bf16[1,512,512]{2,1,0:T(8,128)(2,1)S(1)} copy-done((bf16[1,512,512]{2,1,0:T(8,128)(2,1)S(1)}, bf16[1,512,512]{2,1,0:T(8,128)(2,1)}, u32[]{:S(2)}) %copy-start) | copy-done | bytes 524312
  1.7 0.0 copy-start.1
  1.7 1.0 %copy-done.1 = bf16[1,512,512]{2,1,0:T(8,128)(2,1)S(1)} copy-done((bf16[1,512,512]{2,1,0:T(8,128)(2,1)S(1)}, bf16[1,512,512]{2,1,0:T(8,128)(2,1)}, u32[]{:S(2)}) %copy-start.1) | copy-done | bytes 524312
  2.7 65.4 %shard_map.75 = (bf16[1,512,512]{2,1,0:T(8,128)(2,1)S(1)}, f32[1,512,512]{2,1,0:T(8,128)S(1)}, f32[2,384,256]{2,1,0:T(8,128)S(1)}, f32[2,128,128]{2,1,0:T(8,128)S(1)}) custom-call(bf16[1,512,512]{2,1,0:T(8,128)(2,1)S(1)} %copy-done, bf16[2,1536,1024]{2,1,0:T(8,128)(2,1)} %w_ref.1, bf16[2,512,512]{2,1,0:T(8,128)(2,1)} %r_ref.1, bf16[1,512,512]{2,1,0:T(8,128)(2,1)S(1)} %copy-done.1), custom_call_target="tpu_custom_call" | custom-call | flops 14000000000 | bytes 12000000 | tf_op jit(solution)/shard_map/pallas_call | solution.py:494
  68.2 0.8 %copy.12 = bf16[1,512,512]{2,1,0:T(8,128)(2,1)} copy(bf16[1,512,512]{2,1,0:T(8,128)(2,1)S(1)} %get-tuple-element.8) | data formatting | bytes 1048576
  68.9 1.0 %copy.13 = f32[1,512,512]{2,1,0:T(8,128)} copy(f32[1,512,512]{2,1,0:T(8,128)S(1)} %get-tuple-element.9) | data formatting | bytes 2097152
  69.9 0.9 %copy.14 = f32[2,384,256]{2,1,0:T(8,128)} copy(f32[2,384,256]{2,1,0:T(8,128)S(1)} %get-tuple-element.10) | data formatting | bytes 1572864
  70.8 0.7 copy.15
Async XLA Ops:
  0.6 1.0 %copy-start = (bf16[1,512,512]{2,1,0:T(8,128)(2,1)S(1)}, bf16[1,512,512]{2,1,0:T(8,128)(2,1)}, u32[]{:S(2)}) copy-start(bf16[1,512,512]{2,1,0:T(8,128)(2,1)} %x_ref.1) | copy-start | bytes 1572868
  1.7 1.0 %copy-start.1 = (bf16[1,512,512]{2,1,0:T(8,128)(2,1)S(1)}, bf16[1,512,512]{2,1,0:T(8,128)(2,1)}, u32[]{:S(2)}) copy-start(bf16[1,512,512]{2,1,0:T(8,128)(2,1)} %ct_ref.1) | copy-start | bytes 1572868

commit v2 on v1

--- a/solution.py
+++ b/solution.py
@@ -123,21 +123,22 @@
 def fused_kernel(
     dp_count,
     x_ref, w_ref, r_ref, ct_ref,
-    out_ref, ig_ref, gc_ref, gr_ref,
+    out_ref, ig_ref, gcv, grv,
     sbuf, w0, w1, rw, ctb,
     fa0, fb0, fa1, fb1, z0, z1, s1, dpre, g1, lt,
-    outv, igv, hsend, hrecv,
+    hsend, hrecv,
     acc0, acc1, accr,
     cs0, cr0, cs1, cr1, csr, crr,
-    zs0, zr0, zs1, zr1, zsr, zrr,
-    fs1, fr1, gcv, grv,
-    lsem, osem, ys_s, ys_r, yc_s, yc_r, xs_s, xs_r, fw_s, fw_r, h_s, h_r,
+    zs0, zr0, zs1, zr1, zsr, zrr, rel0, rel1, relr, pre_buf,
+    fs1, fr1,
+    lsem, ys_s, ys_r, yc_s, yc_r, xs_s, xs_r, fw_s, fw_r, h_s, h_r,
     c0_s, c0_r, c1_s, c1_r, cr_s, cr_r,
-    za_s, za_r, zb_s, zb_r, zc_s, zc_r, f_s, f_r,
+    za_s, za_r, zb_s, zb_r, zc_s, zc_r, f_s, f_r, ra_r, rb_r, rc_r,
 ):
     s = lax.axis_index("seq")
     p = lax.axis_index("dp")
     y = s // 2
+    outv, igv = out_ref.at[0], ig_ref.at[0]
     c = s % 2
     other = s + 1 - 2 * c
     across = s + 2 - 4 * y
@@ -149,6 +150,10 @@
     own0 = 3 * chan // 4
     own1 = chan // 4
     ymid = pl.multiple_of(y * (chan // 2), 256)
+    edge = jnp.logical_or(p == 0, p == dp_count - 1)
+    near = jnp.where(p < 2, 3, 1)
+    hops = [near, 4 - near, 2, 0]
+    dest = [(p + hop) % dp_count for hop in hops]
 
     local_copies = [
         pltpu.make_async_copy(x_ref.at[0], sbuf.at[2 + s], lsem.at[0]),
@@ -206,26 +211,31 @@
         copy.wait()
     s_pair.wait_recv()
 
-    def take_over():
-        for h in range(2):
-            s_over[h].wait_recv()
-            s_fwd[h].start()
-        for h in range(2):
-            s_fwd[h].wait_recv()
-
-    pl.when(y == 1)(take_over)
+    def take_over(h):
+        r = pl.ds(pl.multiple_of(h * half, half), half)
+        remote(x_ref.at[0, r], sbuf.at[2 + across, r], ys_s.at[h], ys_r.at[h], {"seq": across}).wait_recv()
+        forwarded = remote(sbuf.at[2 + across, r], sbuf.at[2 + across, r], fw_s.at[h], fw_r.at[h],
+                           {"seq": other})
+        forwarded.start()
+        forwarded.wait_recv()
 
     def forward(k, u):
         def part(h, _):
             r = pl.ds(pl.multiple_of(h * half, half), half)
-            now, back, back2 = sbuf[u + 2, r], sbuf[u + 1, r], sbuf[u, r]
-
-            def pre(lo):
-                return (
-                    mm(now, w0[0:chan, lo : lo + chan])
-                    + mm(back, w0[chan : 2 * chan, lo : lo + chan])
-                    + mm(back2, w0[2 * chan :, lo : lo + chan])
-                )
+            if k == 1:
+                pl.when(y == 0)(lambda: take_over(h))
+            now = sbuf[u + 2, r]
+            pre_buf[...] = mm(now, w0[0:chan])
+            if k == 0:
+                pl.when(y == 1)(lambda: take_over(h))
+
+            @pl.when(u >= 1)
+            def _():
+                pre_buf[...] = pre_buf[...] + mm(sbuf[u + 1, r], w0[chan : 2 * chan])
+
+            @pl.when(u >= 2)
+            def _():
+                pre_buf[...] = pre_buf[...] + mm(sbuf[u, r], w0[2 * chan :])
 
             def gate(filt, sig, fa, fb):
                 f = jnp.tanh(filt)
@@ -235,7 +245,7 @@
                 fb[r] = fg * (1.0 - g)
                 return fg.astype(BF16)
 
-            z = gate(pre(0), pre(chan), fa0, fb0)
+            z = gate(pre_buf[:, 0:chan], pre_buf[:, chan:], fa0, fb0)
             z0[r] = z
             nxt = (now.astype(F32) + mm(z, rw[0])).astype(BF16)
             s1[r] = nxt
@@ -247,8 +257,14 @@
 
         lax.fori_loop(0, 2, part, 0)
 
-    def transposed(u):
-        lt[pl.ds(ymid, chan)] = sbuf[u + 2 * (1 - y)].T
+    def transposed(k, u):
+        def big():
+            lt[pl.ds(ymid, chan)] = sbuf[u + 2 * (1 - y)].T
+
+        if k == 0:
+            big()
+        else:
+            pl.when(y == 0)(big)
         small = sbuf[u + 1, :, pl.ds(ymid, chan // 2)]
         lt[pl.ds(pl.multiple_of((1 - y) * chan, 256), chan // 2)] = small.T
 
@@ -287,7 +303,12 @@
             dpre[r, chan:] = (dz * fb0[r]).astype(BF16)
             return 0
 
-        lax.fori_loop(0, 2, part, 0)
+        if k == 0:
+            lax.fori_loop(0, 2, part, 0)
+        else:
+            @pl.when(s != 2)
+            def _():
+                lax.fori_loop(0, 2, part, 0)
         gr0 = mm_tn(z0[:, pl.ds(ymid, chan // 2)], g1[...].astype(BF16))
         if k == 0:
             accr[0] = gr0
@@ -308,14 +329,11 @@
         lax.fori_loop(0, 2, part, 0)
 
     forward(0, s)
-    out_copy = pltpu.make_async_copy(outv, out_ref.at[0], osem.at[0])
-    out_copy.start()
     back_one(0, s)
     back_zero(0, s)
-    transposed(s)
-    for k in range(dp_count):
-        q = (p + k) % dp_count
-        acc0[k] = mm(lt[...], dpre[:, pl.ds(pl.multiple_of(q * col, col), col)])
+    transposed(0, s)
+    for j in range(dp_count):
+        acc0[j] = mm(lt[...], dpre[:, pl.ds(pl.multiple_of(dest[j] * col, 128), col)])
 
     def direct(r):
         igv[r] = g1[r] + taps_back(0)(r)
@@ -329,9 +347,8 @@
     def _():
         over_halves(lagged)
 
-    pl.when(y == 0)(take_over)
     forward(1, across)
-    transposed(across)
+    transposed(1, across)
     back_one(1, across)
 
     mine1, theirs1 = pl.multiple_of(c * own1, 128), pl.multiple_of((1 - c) * own1, 128)
@@ -349,63 +366,130 @@
 
     back_zero(1, across)
 
-    def spread(k, src, dst, send, recv):
-        return remote(src, dst, send, recv, {"dp": (p + k) % dp_count})
-
-    def send_res(layer):
-        total = accr[layer, pl.ds(mine1, own1)] + crr[layer].astype(F32)
-        accr[layer, pl.ds(mine1, own1)] = total
-        copies = []
-        for k in range(1, dp_count):
-            q = (p + k) % dp_count
-            part = accr[layer, pl.ds(mine1, own1), pl.ds(pl.multiple_of(q * rcol, rcol), rcol)]
-            zsr[layer, k - 1] = part.astype(BF16)
-            copy = spread(k, zsr.at[layer, k - 1], zrr.at[layer, k - 1], zc_s.at[layer, k - 1],
-                          zc_r.at[layer, k - 1])
-            copy.start()
-            copies.append(copy)
-        return copies
-
-    pair1.wait_recv()
-    acc1[pl.ds(mine1, own1)] = acc1[pl.ds(mine1, own1)] + cr1[...].astype(F32)
-    over1 = []
-    for k in range(1, dp_count):
-        q = (p + k) % dp_count
-        part = acc1[pl.ds(mine1, own1), pl.ds(pl.multiple_of(q * col, col), col)]
-        zs1[k - 1] = part.astype(BF16)
-        copy = spread(k, zs1.at[k - 1], zr1.at[k - 1], zb_s.at[k - 1], zb_r.at[k - 1])
+    def along(j, src, dst, send, recv):
+        slot = hops[j] - 1
+        return remote(src.at[j], dst.at[slot], send.at[j], recv.at[slot], {"dp": dest[j]})
+
+    def out_first(src, dst, relay, send, recv, relay_recv):
+        direct = along(0, src, dst, send, recv)
+        handed = remote(src.at[0], relay, send.at[0], relay_recv, {"dp": dest[1]})
+        pl.when(jnp.logical_not(edge))(direct.start)
+        pl.when(edge)(handed.start)
+        return direct, handed
+
+    def out_last(total, src, dst, relay, send, recv, handed):
+        copy = along(2, src, dst, send, recv)
+
+        @pl.when(edge)
+        def _():
+            src[2] = total.astype(BF16)
+
+        @pl.when(jnp.logical_not(edge))
+        def _():
+            handed.wait_recv()
+            src[2] = (total + relay[...].astype(F32)).astype(BF16)
+
         copy.start()
-        over1.append(copy)
-    pair_r1.wait_recv()
-    over_r1 = send_res(1)
+        return copy
+
+    def gather_in(total, dst, home):
+        home[...] = total + dst[1].astype(F32)
+
+        @pl.when(p != 0)
+        def _():
+            home[...] = home[...] + dst[0].astype(F32)
+
+        @pl.when(p != dp_count - 1)
+        def _():
+            home[...] = home[...] + dst[2].astype(F32)
+
+    def arrived(src, dst, send, recv):
+        def one(slot):
+            return remote(src.at[0], dst.at[slot], send.at[0], recv.at[slot], {"dp": dest[1]})
+
+        one(1).wait_recv()
+        pl.when(p != 0)(one(0).wait_recv)
+        pl.when(p != dp_count - 1)(one(2).wait_recv)
+
+    def cols(j, size):
+        return pl.ds(pl.multiple_of(dest[j] * size, 128), size)
+
+    first = {}
+    last = []
+    m1 = pl.ds(mine1, own1)
+
+    def start_one():
+        pair1.wait_recv()
+        acc1[m1] = acc1[m1] + cr1[...].astype(F32)
+        for j in range(2):
+            zs1[j] = acc1[m1, cols(j, col)].astype(BF16)
+        first["1"] = out_first(zs1, zr1, rel1, zb_s, zb_r, rb_r)
+        copy = along(1, zs1, zr1, zb_s, zb_r)
+        copy.start()
+        last.append(copy)
+
+    def start_res(layer, pair):
+        pair.wait_recv()
+        accr[layer, m1] = accr[layer, m1] + crr[layer].astype(F32)
+        for j in range(2):
+            zsr[layer, j] = accr[layer, m1, cols(j, rcol)].astype(BF16)
+        first[layer] = out_first(zsr.at[layer], zrr.at[layer], relr.at[layer], zc_s.at[layer],
+                                 zc_r.at[layer], rc_r.at[layer])
+        copy = along(1, zsr.at[layer], zrr.at[layer], zc_s.at[layer], zc_r.at[layer])
+        copy.start()
+        last.append(copy)
+
+    def end_one():
+        last.append(out_last(acc1[m1, cols(2, col)], zs1, zr1, rel1, zb_s, zb_r, first["1"][1]))
+
+    def end_res(layer):
+        last.append(out_last(accr[layer, m1, cols(2, rcol)], zsr.at[layer], zrr.at[layer],
+                             relr.at[layer], zc_s.at[layer], zc_r.at[layer], first[layer][1]))
+
+    start_one()
+    start_res(1, pair_r1)
 
     csr[0] = accr[0, pl.ds(theirs1, own1)].astype(BF16)
     pair_r0 = pair_res(0)
     pair_r0.start()
 
-    order = list(range(1, dp_count)) + [0]
-    pairs0 = {}
-    over0 = []
-
-    def pass_on(k):
-        pairs0[k].wait_recv()
-        if k == 0:
-            return
-        zs0[k - 1] = (acc0[k, pl.ds(mine0, own0)] + cr0[k].astype(F32)).astype(BF16)
-        copy = spread(k, zs0.at[k - 1], zr0.at[k - 1], za_s.at[k - 1], za_r.at[k - 1])
-        copy.start()
-        over0.append(copy)
-
-    for place, k in enumerate(order):
-        q = (p + k) % dp_count
-        acc0[k] = acc0[k] + mm(lt[...], dpre[:, pl.ds(pl.multiple_of(q * col, col), col)])
-        cs0[k] = acc0[k, pl.ds(theirs0, own0)].astype(BF16)
-        pairs0[k] = remote(cs0.at[k], cr0.at[k], c0_s.at[k], c0_r.at[k], {"seq": other})
-        pairs0[k].start()
-        if place > 0:
-            pass_on(order[place - 1])
-    pair_r0.wait_recv()
-    over_r0 = send_res(0)
+    pairs0 = []
+    m0 = pl.ds(mine0, own0)
+
+    def pass_on(j):
+        pairs0[j].wait_recv()
+        total = acc0[j, m0] + cr0[j].astype(F32)
+        if j < 2:
+            zs0[j] = total.astype(BF16)
+        if j == 0:
+            first["0"] = out_first(zs0, zr0, rel0, za_s, za_r, ra_r)
+        elif j == 1:
+            copy = along(1, zs0, zr0, za_s, za_r)
+            copy.start()
+            last.append(copy)
+        elif j == 2:
+            last.append(out_last(total, zs0, zr0, rel0, za_s, za_r, first["0"][1]))
+
+    for j in range(dp_count):
+        @pl.when(y == 0)
+        def _():
+            acc0[j] = acc0[j] + mm(lt[...], dpre[:, cols(j, col)])
+
+        @pl.when(s == 3)
+        def _():
+            small = pl.ds(0, chan // 2)
+            acc0[j, small] = acc0[j, small] + mm(lt[small], dpre[:, cols(j, col)])
+
+        cs0[j] = acc0[j, pl.ds(theirs0, own0)].astype(BF16)
+        pairs0.append(remote(cs0.at[j], cr0.at[j], c0_s.at[j], c0_r.at[j], {"seq": other}))
+        pairs0[j].start()
+        if j == 1:
+            pass_on(0)
+            end_one()
+            end_res(1)
+        if j == 2:
+            pass_on(1)
+    start_res(0, pair_r0)
 
     @pl.when(jnp.logical_and(c == 0, y == 0))
     def _():
@@ -421,19 +505,14 @@
     def _():
         over_halves(lagged_twice)
 
-    pass_on(0)
+    pass_on(2)
+    end_res(0)
+    pass_on(3)
     pair_h.wait_recv()
     igv[...] = igv[...] + hrecv[...].astype(F32)
-    ig_copy = pltpu.make_async_copy(igv, ig_ref.at[0], osem.at[1])
-    ig_copy.start()
-
-    for copy in over1:
-        copy.wait_recv()
-    here = pl.ds(pl.multiple_of(p * col, col), col)
-    total1 = acc1[pl.ds(mine1, own1), here]
-    for k in range(dp_count - 1):
-        total1 = total1 + zr1[k].astype(F32)
-    fs1[...] = total1
+
+    arrived(zs1, zr1, zb_s, zb_r)
+    gather_in(acc1[m1, cols(3, col)], zr1, fs1)
 
     to_first = remote(fs1, fr1.at[0], f_s, f_r.at[0], {"seq": 0})
     to_first2 = remote(fs1, fr1.at[1], f_s, f_r.at[1], {"seq": 0})
@@ -442,15 +521,9 @@
     pl.when(s == 2)(to_first2.start)
     pl.when(s == 3)(to_second.start)
 
-    for layer, copies in ((1, over_r1), (0, over_r0)):
-        for copy in copies:
-            copy.wait_recv()
-        total = accr[layer, pl.ds(mine1, own1), pl.ds(pl.multiple_of(p * rcol, rcol), rcol)]
-        for k in range(dp_count - 1):
-            total = total + zrr[layer, k].astype(F32)
-        grv[layer] = total
-    gr_copy = pltpu.make_async_copy(grv, gr_ref, osem.at[2])
-    gr_copy.start()
+    for layer in (1, 0):
+        arrived(zsr.at[layer], zrr.at[layer], zc_s.at[layer], zc_r.at[layer])
+        gather_in(accr[layer, m1, cols(3, rcol)], zrr.at[layer], grv.at[layer])
 
     gcv[1] = jnp.zeros((own0, col), F32)
 
@@ -467,21 +540,14 @@
         to_second.wait_recv()
         gcv[1, 0:own1] = fr1[0]
 
-    total0 = acc0[0, pl.ds(mine0, own0)] + cr0[0].astype(F32)
-    for k in range(dp_count - 1):
-        over0[k].wait_recv()
-        total0 = total0 + zr0[k].astype(F32)
-    gcv[0] = total0
-    gc_copy = pltpu.make_async_copy(gcv, gc_ref, osem.at[3])
-    gc_copy.start()
+    arrived(zs0, zr0, za_s, za_r)
+    gather_in(acc0[3, m0] + cr0[3].astype(F32), zr0, gcv.at[0])
 
     for copy in s_over + c_over + [s_pair] + s_fwd + [pair1, pair_r1, pair_r0, pair_h]:
         copy.wait_send()
-    for copy in list(pairs0.values()) + over1 + over_r1 + over_r0 + over0:
+    for copy in pairs0 + last + [direct for direct, handed in first.values()]:
         copy.wait_send()
     pl.when(s > 0)(to_first.wait_send)
-    for copy in (out_copy, ig_copy, gr_copy, gc_copy):
-        copy.wait()
 
 
 def fused(dp_count, stream_in, conv_weight, res_weight, out_cotangent):
@@ -499,8 +565,8 @@
             jax.ShapeDtypeStruct((2, own0, col), F32),
             jax.ShapeDtypeStruct((2, own1, rcol), F32),
         ),
-        in_specs=[pl.BlockSpec(memory_space=pl.ANY)] * 4,
-        out_specs=(pl.BlockSpec(memory_space=pl.ANY),) * 4,
+        in_specs=[pl.BlockSpec(memory_space=pltpu.HBM)] * 4,
+        out_specs=(pl.BlockSpec(memory_space=pltpu.VMEM),) * 4,
         scratch_shapes=[
             v((6, length, chan), BF16), v((3 * chan, width), BF16), v((chan, width), BF16),
             v((2, chan, chan), BF16), v((2, length, chan), BF16),
@@ -508,7 +574,6 @@
             v((length, chan), F32), v((length, chan), BF16), v((length, chan), BF16),
             v((length, chan), BF16), v((length, width), BF16), v((length, chan), F32),
             v((3 * chan // 2, length), BF16),
-            v((length, chan), BF16), v((length, chan), F32),
             v((length, chan), BF16), v((length, chan), BF16),
             v((dp_count, 2 * own0, col), F32), v((2 * own1, width), F32), v((2, 2 * own1, chan), F32),
             v((dp_count, own0, col), BF16), v((dp_count, own0, col), BF16),
@@ -517,13 +582,14 @@
             v((away, own0, col), BF16), v((away, own0, col), BF16),
             v((away, own1, col), BF16), v((away, own1, col), BF16),
             v((2, away, own1, rcol), BF16), v((2, away, own1, rcol), BF16),
+            v((own0, col), BF16), v((own1, col), BF16), v((2, own1, rcol), BF16),
+            v((length // 2, width), F32),
             v((own1, col), F32), v((2, own1, col), F32),
-            v((2, own0, col), F32), v((2, own1, rcol), F32),
-            dma((5,)), dma((4,)), dma((2,)), dma((2,)), dma((2,)), dma((2,)), dma, dma,
+            dma((5,)), dma((2,)), dma((2,)), dma((2,)), dma((2,)), dma, dma,
             dma((2,)), dma((2,)), dma, dma,
             dma((dp_count,)), dma((dp_count,)), dma, dma, dma((2,)), dma((2,)),
             dma((away,)), dma((away,)), dma((away,)), dma((away,)),
-            dma((2, away)), dma((2, away)), dma, dma((2,)),
+            dma((2, away)), dma((2, away)), dma, dma((2,)), dma, dma, dma((2,)),
         ],
         compiler_params=pltpu.CompilerParams(
             collective_id=0, has_side_effects=True, vmem_limit_bytes=50 * 1024 * 1024

time: 71.7 us -> 64.8 us (0.904)
  Pallas kernels: 65.4 us -> 58.6 us
    pallas_call x1, Pallas kernels: 65.4 us -> 58.6 us  [fused(): pl.pallas_call(functools.partial(fused_kernel, dp_count), out_shape=(jax....]
where the time goes in v2:
time: 64.8 us; the launch traced here: 64.6 us
  Pallas kernels  58.6 us (90%)
  local copies, waits for them, and re-layouts  5.37 us (8%)
  between operations  0.65 us (1%)
    pallas_call x1, Pallas kernels, fused(): pl.pallas_call(functools.partial(fused_kernel, dp_count), out_shape=(jax....  58.6 us
    unnamed x8, local copies, waits for them, and re-layouts  5.37 us

profile of v2, /device:TPU:4, one launch (start us, length us, event | category | flops | bytes accessed | tf_op | source)
XLA Modules:
  0.0 64.6 jit_solution(15052385986202519122)
XLA Ops:
  0.6 0.0 copy-start
  0.6 1.0 %copy-done = bf16[1,512,512]{2,1,0:T(8,128)(2,1)S(1)} copy-done((bf16[1,512,512]{2,1,0:T(8,128)(2,1)S(1)}, bf16[1,512,512]{2,1,0:T(8,128)(2,1)}, u32[]{:S(2)}) %copy-start) | copy-done | bytes 524312
  1.7 0.0 copy-start.1
  1.7 1.0 %copy-done.1 = bf16[1,512,512]{2,1,0:T(8,128)(2,1)S(1)} copy-done((bf16[1,512,512]{2,1,0:T(8,128)(2,1)S(1)}, bf16[1,512,512]{2,1,0:T(8,128)(2,1)}, u32[]{:S(2)}) %copy-start.1) | copy-done | bytes 524312
  2.7 58.6 %shard_map.75 = (bf16[1,512,512]{2,1,0:T(8,128)(2,1)S(1)}, f32[1,512,512]{2,1,0:T(8,128)S(1)}, f32[2,384,256]{2,1,0:T(8,128)S(1)}, f32[2,128,128]{2,1,0:T(8,128)S(1)}) custom-call(bf16[1,512,512]{2,1,0:T(8,128)(2,1)S(1)} %copy-done, bf16[2,1536,1024]{2,1,0:T(8,128)(2,1)} %w_ref.1, bf16[2,512,512]{2,1,0:T(8,128)(2,1)} %r_ref.1, bf16[1,512,512]{2,1,0:T(8,128)(2,1)S(1)} %copy-done.1), custom_call_target="tpu_custom_call" | custom-call | flops 14000000000 | bytes 12000000 | tf_op jit(solution)/shard_map/pallas_call | solution.py:560
  61.3 0.8 %copy.12 = bf16[1,512,512]{2,1,0:T(8,128)(2,1)} copy(bf16[1,512,512]{2,1,0:T(8,128)(2,1)S(1)} %get-tuple-element.8) | data formatting | bytes 1048576
  62.1 1.0 %copy.13 = f32[1,512,512]{2,1,0:T(8,128)} copy(f32[1,512,512]{2,1,0:T(8,128)S(1)} %get-tuple-element.9) | data formatting | bytes 2097152
  63.1 0.9 %copy.14 = f32[2,384,256]{2,1,0:T(8,128)} copy(f32[2,384,256]{2,1,0:T(8,128)S(1)} %get-tuple-element.10) | data formatting | bytes 1572864
  64.0 0.7 %copy.15 = f32[2,128,128]{2,1,0:T(8,128)} copy(f32[2,128,128]{2,1,0:T(8,128)S(1)} %get-tuple-element.11) | data formatting | bytes 262144
Async XLA Ops:
  0.6 1.0 %copy-start = (bf16[1,512,512]{2,1,0:T(8,128)(2,1)S(1)}, bf16[1,512,512]{2,1,0:T(8,128)(2,1)}, u32[]{:S(2)}) copy-start(bf16[1,512,512]{2,1,0:T(8,128)(2,1)} %x_ref.1) | copy-start | bytes 1572868
  1.7 1.0 %copy-start.1 = (bf16[1,512,512]{2,1,0:T(8,128)(2,1)S(1)}, bf16[1,512,512]{2,1,0:T(8,128)(2,1)}, u32[]{:S(2)}) copy-start(bf16[1,512,512]{2,1,0:T(8,128)(2,1)} %ct_ref.1) | copy-start | bytes 1572868

commit v3 on v2

--- a/solution.py
+++ b/solution.py
@@ -295,7 +295,7 @@
             accr[1] = accr[1] + gr1
             acc1[...] = acc1[...] + gc1
 
-    def back_zero(k, u):
+    def back_zero(k, u, between=None):
         def part(h, _):
             r = pl.ds(pl.multiple_of(h * half, half), half)
             dz = mm_nt(g1[r].astype(BF16), rw[0])
@@ -306,9 +306,12 @@
         if k == 0:
             lax.fori_loop(0, 2, part, 0)
         else:
-            @pl.when(s != 2)
-            def _():
-                lax.fori_loop(0, 2, part, 0)
+            for h in range(2):
+                @pl.when(s != 2)
+                def _():
+                    lax.fori_loop(h, h + 1, part, 0)
+
+                between[h]()
         gr0 = mm_tn(z0[:, pl.ds(ymid, chan // 2)], g1[...].astype(BF16))
         if k == 0:
             accr[0] = gr0
@@ -364,7 +367,6 @@
     pair_r1 = pair_res(1)
     pair_r1.start()
 
-    back_zero(1, across)
 
     def along(j, src, dst, send, recv):
         slot = hops[j] - 1
@@ -446,8 +448,7 @@
         last.append(out_last(accr[layer, m1, cols(2, rcol)], zsr.at[layer], zrr.at[layer],
                              relr.at[layer], zc_s.at[layer], zc_r.at[layer], first[layer][1]))
 
-    start_one()
-    start_res(1, pair_r1)
+    back_zero(1, across, (start_one, lambda: start_res(1, pair_r1)))
 
     csr[0] = accr[0, pl.ds(theirs1, own1)].astype(BF16)
     pair_r0 = pair_res(0)
@@ -498,6 +499,9 @@
     pair_h = remote(hsend, hrecv, h_s, h_r, {"seq": other})
     pair_h.start()
 
+    pass_on(2)
+    end_res(0)
+
     def lagged_twice(r):
         igv[r] = igv[r] + taps_back(2)(r)
 
@@ -505,8 +509,6 @@
     def _():
         over_halves(lagged_twice)
 
-    pass_on(2)
-    end_res(0)
     pass_on(3)
     pair_h.wait_recv()
     igv[...] = igv[...] + hrecv[...].astype(F32)

time: 64.8 us -> 63.8 us (0.985)
  Pallas kernels: 58.6 us -> 57.4 us
    pallas_call x1, Pallas kernels: 58.6 us -> 57.4 us  [fused(): pl.pallas_call(functools.partial(fused_kernel, dp_count), out_shape=(jax....]
where the time goes in v3:
time: 63.8 us; the launch traced here: 63.4 us
  Pallas kernels  57.4 us (90%)
  local copies, waits for them, and re-layouts  5.37 us (8%)
  between operations  0.65 us (1%)
    pallas_call x1, Pallas kernels, fused(): pl.pallas_call(functools.partial(fused_kernel, dp_count), out_shape=(jax....  57.4 us
    unnamed x8, local copies, waits for them, and re-layouts  5.37 us

profile of v3, /device:TPU:4, one launch (start us, length us, event | category | flops | bytes accessed | tf_op | source)
XLA Modules:
  0.0 63.4 jit_solution(3955887637375019010)
XLA Ops:
  0.6 0.0 copy-start
  0.6 1.0 %copy-done = bf16[1,512,512]{2,1,0:T(8,128)(2,1)S(1)} copy-done((bf16[1,512,512]{2,1,0:T(8,128)(2,1)S(1)}, bf16[1,512,512]{2,1,0:T(8,128)(2,1)}, u32[]{:S(2)}) %copy-start) | copy-done | bytes 524312
  1.7 0.0 copy-start.1
  1.7 1.0 %copy-done.1 = bf16[1,512,512]{2,1,0:T(8,128)(2,1)S(1)} copy-done((bf16[1,512,512]{2,1,0:T(8,128)(2,1)S(1)}, bf16[1,512,512]{2,1,0:T(8,128)(2,1)}, u32[]{:S(2)}) %copy-start.1) | copy-done | bytes 524312
  2.7 57.4 %shard_map.75 = (bf16[1,512,512]{2,1,0:T(8,128)(2,1)S(1)}, f32[1,512,512]{2,1,0:T(8,128)S(1)}, f32[2,384,256]{2,1,0:T(8,128)S(1)}, f32[2,128,128]{2,1,0:T(8,128)S(1)}) custom-call(bf16[1,512,512]{2,1,0:T(8,128)(2,1)S(1)} %copy-done, bf16[2,1536,1024]{2,1,0:T(8,128)(2,1)} %w_ref.1, bf16[2,512,512]{2,1,0:T(8,128)(2,1)} %r_ref.1, bf16[1,512,512]{2,1,0:T(8,128)(2,1)S(1)} %copy-done.1), custom_call_target="tpu_custom_call" | custom-call | flops 14000000000 | bytes 12000000 | tf_op jit(solution)/shard_map/pallas_call | solution.py:562
  60.1 0.8 %copy.12 = bf16[1,512,512]{2,1,0:T(8,128)(2,1)} copy(bf16[1,512,512]{2,1,0:T(8,128)(2,1)S(1)} %get-tuple-element.8) | data formatting | bytes 1048576
  60.9 1.0 %copy.13 = f32[1,512,512]{2,1,0:T(8,128)} copy(f32[1,512,512]{2,1,0:T(8,128)S(1)} %get-tuple-element.9) | data formatting | bytes 2097152
  61.9 0.9 %copy.14 = f32[2,384,256]{2,1,0:T(8,128)} copy(f32[2,384,256]{2,1,0:T(8,128)S(1)} %get-tuple-element.10) | data formatting | bytes 1572864
  62.7 0.7 %copy.15 = f32[2,128,128]{2,1,0:T(8,128)} copy(f32[2,128,128]{2,1,0:T(8,128)S(1)} %get-tuple-element.11) | data formatting | bytes 262144
Async XLA Ops:
  0.6 1.0 %copy-start = (bf16[1,512,512]{2,1,0:T(8,128)(2,1)S(1)}, bf16[1,512,512]{2,1,0:T(8,128)(2,1)}, u32[]{:S(2)}) copy-start(bf16[1,512,512]{2,1,0:T(8,128)(2,1)} %x_ref.1) | copy-start | bytes 1572868
  1.7 1.0 %copy-start.1 = (bf16[1,512,512]{2,1,0:T(8,128)(2,1)S(1)}, bf16[1,512,512]{2,1,0:T(8,128)(2,1)}, u32[]{:S(2)}) copy-start(bf16[1,512,512]{2,1,0:T(8,128)(2,1)} %ct_ref.1) | copy-start | bytes 1572868
